TPU v7x, 512 devices: a whole 4x8x8 slice. The times are simulated.
512 devices in a mesh: grp: 8 (over y), row: 8 (over z), col: 8 (over x, core).
Axes of the slice: x: 4, y: 8, z: 8, core: 2. Of those that a mesh axis runs over, the one named last changes fastest.
Arguments:
- new_rows: bfloat16 [768, 16, 8192], P(('grp', 'col'), None, 'row'), may hold values from -6 to 6
- query_weight: bfloat16 [8192, 8192], P('row', 'col')
- key_weight: bfloat16 [8192, 1024], P('row', 'col')
- value_weight: bfloat16 [8192, 1024], P('row', 'col'), may hold values from -0.0625 to 0.0625
- cache_keys: bfloat16 [768, 512, 1024], P(('grp', 'row'), None, 'col'), may hold values from -6 to 6
- cache_values: bfloat16 [768, 512, 1024], P(('grp', 'row'), None, 'col'), may hold values from -6 to 6
- region_agents: int32 [768], replicated, may hold values from 0 to 767, as said below
- new_counts: int32 [768], replicated, may hold values from 4 to 16, as said below
- cache_lengths: int32 [768], replicated, may hold values from 1 to 512, as said below
Outputs:
- attended: bfloat16 [768, 16, 8192], P(('grp', 'col'), 'row')
Inputs may be any that keep to these rules, and one draw needn't show every extreme that they name: `region_agents`: A permutation of the 768 agents. Rows i with equal i // 12 form one region; agent a is served by group a // 96. Every region holds at most 3 agents served by one group, and exactly 3 of some group. `new_counts`: some agent has 16 new tokens. `cache_lengths`: some agent has 512 cached positions.
All inputs are finite; a program needn't handle non-finite values.
Results may differ from a plain program's by a relative error of at most 0.025.
Values may be sent and summed in bfloat16 or wider, within the bound.
A program may use at most 64 MiB of HBM per device.

v0:
```python
import jax
import jax.numpy as jnp
from jax import lax
from jax.sharding import PartitionSpec as P

HEAD_DIM = 128
rotary_base = 500000.0
floor_score = -1e30


def rotate_pairs(values, positions):
    half_dim = values.shape[-1] // 2
    exponent = jnp.arange(half_dim, dtype=jnp.float32) * (2.0 / values.shape[-1])
    frequency = rotary_base ** (-exponent)
    angles = positions.astype(jnp.float32)[..., None, None] * frequency
    cosine = jnp.cos(angles)
    sine_part = jnp.sin(angles)
    first_half = values[..., :half_dim]
    second = values[..., half_dim:]
    return jnp.concatenate(
        [first_half * cosine - second * sine_part, second * cosine + first_half * sine_part],
        axis=-1,
    )


def local(
    new_rows,
    query_weight,
    key_weight,
    value_weight,
    cache_keys,
    cache_values,
    region_agents,
    new_counts,
    cache_lengths,
):
    groups = lax.axis_size("grp")
    grid_rows = lax.axis_size("row")
    grid_cols = lax.axis_size("col")
    group_index = lax.axis_index("grp")
    row_index = lax.axis_index("row")
    col_index = lax.axis_index("col")
    agents_total = region_agents.shape[0]
    per_group = agents_total // groups
    per_region = new_rows.shape[0]
    regions = groups * grid_cols
    capacity = max(2, 2 * per_region // groups)
    slot_count = new_rows.shape[1]
    feature_width = new_rows.shape[2]
    slot_width = slot_count // grid_cols
    served_by = region_agents // per_group
    grouped = served_by.reshape(regions, per_region)
    earlier = jnp.arange(per_region)[:, None] > jnp.arange(per_region)[None, :]
    same_group = grouped[:, :, None] == grouped[:, None, :]
    bucket = jnp.sum((same_group & earlier[None, :, :]).astype(jnp.int32), axis=2).reshape(
        agents_total
    )
    slot_of_agent = jnp.argsort(region_agents)
    my_region = group_index * grid_cols + col_index
    mine_group = lax.dynamic_slice_in_dim(served_by, my_region * per_region, per_region)
    mine_bucket = lax.dynamic_slice_in_dim(bucket, my_region * per_region, per_region)
    choose = (
        (mine_group[None, None, :] == jnp.arange(groups)[:, None, None])
        & (mine_bucket[None, None, :] == jnp.arange(capacity)[None, :, None])
    ).astype(jnp.bfloat16)
    pieces = new_rows.reshape(per_region, grid_cols, slot_width, feature_width)
    outgoing = jnp.einsum(
        "gkj,jcsd->gcksd", choose, pieces, preferred_element_type=jnp.float32
    ).astype(jnp.bfloat16)
    arrived = lax.all_to_all(
        outgoing.reshape(regions, capacity, slot_width, feature_width),
        ("grp", "col"),
        split_axis=0,
        concat_axis=0,
        tiled=True,
    )
    my_slots = lax.dynamic_slice_in_dim(slot_of_agent, group_index * per_group, per_group)
    source_row = my_slots // per_region * capacity + jnp.take(bucket, my_slots)
    landed = jnp.take(
        arrived.reshape(regions * capacity, slot_width, feature_width), source_row, axis=0
    )
    tokens = lax.all_gather(landed, "col", axis=1, tiled=True)
    agents_here = cache_keys.shape[0]
    picked = tokens.reshape(lax.axis_size("row") * agents_here * slot_count, feature_width)
    query_part = jnp.dot(picked, query_weight, preferred_element_type=jnp.float32)
    key_part = jnp.dot(picked, key_weight, preferred_element_type=jnp.float32)
    value_part = jnp.dot(picked, value_weight, preferred_element_type=jnp.float32)
    summed = lax.psum_scatter(
        jnp.concatenate([query_part, key_part, value_part], axis=1)
        .reshape(lax.axis_size("row") * agents_here, slot_count, -1)
        .astype(jnp.bfloat16),
        "row",
        scatter_dimension=0,
        tiled=True,
    ).astype(jnp.float32)
    local_agents = (
        group_index * per_group + row_index * agents_here + jnp.arange(agents_here, dtype=jnp.int32)
    )
    lengths_now = jnp.take(cache_lengths, local_agents)
    counts_now = jnp.take(new_counts, local_agents)
    positions = lengths_now[:, None] + jnp.arange(slot_count, dtype=jnp.int32)[None, :]
    query_width = query_weight.shape[1]
    key_width = key_weight.shape[1]
    heads_here = query_width // HEAD_DIM
    kv_here = key_width // HEAD_DIM
    group_ratio = heads_here // kv_here
    queries = rotate_pairs(
        summed[:, :, :query_width].reshape(agents_here, slot_count, heads_here, HEAD_DIM), positions
    ).astype(jnp.bfloat16)
    fresh_keys = rotate_pairs(
        summed[:, :, query_width : query_width + key_width].reshape(
            agents_here, slot_count, kv_here, HEAD_DIM
        ),
        positions,
    ).astype(jnp.bfloat16)
    fresh_values = (
        summed[:, :, query_width + key_width :]
        .reshape(agents_here, slot_count, kv_here, HEAD_DIM)
        .astype(jnp.bfloat16)
    )
    query_rows = (
        queries.reshape(agents_here, slot_count, kv_here, group_ratio, HEAD_DIM)
        .transpose(0, 2, 3, 1, 4)
        .reshape(agents_here, kv_here, group_ratio * slot_count, HEAD_DIM)
    )
    cache_span = cache_keys.shape[1]
    stored_keys = cache_keys.reshape(agents_here, cache_span, kv_here, HEAD_DIM)
    stored_values = cache_values.reshape(agents_here, cache_span, kv_here, HEAD_DIM)
    score_scale = HEAD_DIM ** (-0.5)
    slot_of_row = jnp.arange(group_ratio * slot_count, dtype=jnp.int32) % slot_count
    fresh_index = jnp.arange(slot_count, dtype=jnp.int32)
    new_allowed = (
        (fresh_index[None, :] <= slot_of_row[:, None])[None, :, :]
        & (fresh_index[None, None, :] < counts_now[:, None, None])
    )[:, None, :, :]
    new_scores = (
        jnp.einsum("akrd,atkd->akrt", query_rows, fresh_keys, preferred_element_type=jnp.float32)
        * score_scale
    )
    cache_scores = (
        jnp.einsum("akrd,apkd->akrp", query_rows, stored_keys, preferred_element_type=jnp.float32)
        * score_scale
    )
    cache_allowed = (jnp.arange(cache_span, dtype=jnp.int32)[None, :] < lengths_now[:, None])[
        :, None, None, :
    ]
    cache_masked = jnp.where(cache_allowed, cache_scores, floor_score)
    new_masked = jnp.where(new_allowed, new_scores, floor_score)
    row_max = jnp.maximum(jnp.max(cache_masked, axis=3), jnp.max(new_masked, axis=3))
    cache_weights = jnp.where(cache_allowed, jnp.exp(cache_masked - row_max[..., None]), 0.0)
    new_weights = jnp.where(new_allowed, jnp.exp(new_masked - row_max[..., None]), 0.0)
    denominator = jnp.sum(cache_weights, axis=3) + jnp.sum(new_weights, axis=3)
    weighted = jnp.einsum(
        "akrp,apkd->akrd",
        cache_weights.astype(jnp.bfloat16),
        stored_values,
        preferred_element_type=jnp.float32,
    )
    weighted = weighted + jnp.einsum(
        "akrp,apkd->akrd",
        new_weights.astype(jnp.bfloat16),
        fresh_values,
        preferred_element_type=jnp.float32,
    )
    result = (
        (weighted / denominator[..., None])
        .reshape(agents_here, kv_here, group_ratio, slot_count, HEAD_DIM)
        .transpose(0, 3, 1, 2, 4)
        .reshape(agents_here, slot_count, query_width)
    )
    valid_slot = jnp.arange(slot_count, dtype=jnp.int32)[None, :] < counts_now[:, None]
    result = jnp.where(valid_slot[:, :, None], result, 0.0).astype(jnp.bfloat16)
    regrouped = lax.all_to_all(result, "row", split_axis=1, concat_axis=0, tiled=True)
    slot_share = slot_count // grid_rows
    choose_back = (
        jnp.arange(regions * capacity, dtype=jnp.int32)[:, None] == source_row[None, :]
    ).astype(jnp.bfloat16)
    returning = jnp.einsum(
        "qt,tsf->qsf", choose_back, regrouped, preferred_element_type=jnp.float32
    ).astype(jnp.bfloat16)
    incoming = lax.all_to_all(
        returning.reshape(regions, capacity, slot_share, query_width),
        ("grp", "col"),
        split_axis=0,
        concat_axis=0,
        tiled=True,
    ).reshape(groups, grid_cols, capacity, slot_share, query_width)
    select_back = (
        (mine_group[:, None, None] == jnp.arange(groups)[None, :, None])
        & (mine_bucket[:, None, None] == jnp.arange(capacity)[None, None, :])
    ).astype(jnp.bfloat16)
    finished = jnp.einsum(
        "jgk,gcksf->jscf", select_back, incoming, preferred_element_type=jnp.float32
    ).astype(jnp.bfloat16)
    return finished.reshape(per_region, slot_share, grid_cols * query_width)


def solution(mesh):
    placed = (
        P(("grp", "col"), None, "row"),
        P("row", "col"),
        P("row", "col"),
        P("row", "col"),
        P(("grp", "row"), None, "col"),
        P(("grp", "row"), None, "col"),
        P(),
        P(),
        P(),
    )
    return jax.shard_map(
        local, mesh=mesh, in_specs=placed, out_specs=P(("grp", "col"), "row", None), check_vma=False
    )
```

profile of v0, /device:TPU:1, one launch (start us, length us, event | category | flops | bytes accessed | tf_op | source)
XLA Modules:
  0.0 230.3 jit_solution(6798773412891268803)
XLA Ops:
  6.5 0.8 add_select_fusion
  7.4 0.1 eq.103
  7.5 0.1 copy.72
  7.6 0.1 convert_reduce_fusion
  7.7 0.1 copy.74
  7.8 0.1 reshape.407
  7.9 0.1 dynamic_slice.10
  8.0 0.1 dynamic_slice.11
  8.1 1.2 copy.95
  9.3 0.3 fusion.11
  9.7 0.4 copy.122
  10.1 1.7 copy.77
  11.8 11.6 %all-to-all-start = ((bf16[64,3,2,1024]{3,2,1,0:T(2,128)(2,1)}), bf16[64,3,2,1024]{3,2,1,0:T(2,128)(2,1)S(1)}, u32[]{:S(2)}, u32[]{:S(2)}) async-start(bf16[64,3,2,1024]{3,2,1,0:T(2,128)(2,1)} %copy.77), calls=%async_computation | async-start | bytes 1572864 | tf_op jit(solution)/shard_map/all_to_all | solution.py:70
  23.5 4.4 %sort.17 = (s32[768]{0:T(1024)}, s32[768]{0:T(1024)S(1)}) sort(s32[768]{0:T(1024)S(1)} %copy-done.7, s32[768]{0:T(1024)S(1)} %iota.103), dimensions={0}, to_apply=%region_0.1 | sort | flops 7680 | bytes 12288 | tf_op jit(solution)/shard_map/jit(argsort)/sort | solution.py:58
  27.9 0.1 compare_select_fusion.2
  27.9 1.0 gather_fusion
  28.9 0.1 compare_and_fusion.1
  29.0 17.1 %all-to-all-done = bf16[64,3,2,1024]{3,2,1,0:T(2,128)(2,1)S(1)} async-done(((bf16[64,3,2,1024]{3,2,1,0:T(2,128)(2,1)}), bf16[64,3,2,1024]{3,2,1,0:T(2,128)(2,1)S(1)}, u32[]{:S(2)}, u32[]{:S(2)}) %all-to-all-start) | async-done | bytes 786464 | tf_op jit(solution)/shard_map/all_to_all | solution.py:70
  46.2 1.4 gather_fusion.1
  47.5 0.5 broadcast_select_fusion
  48.0 0.8 copy.78
  48.8 0.2 reduce-scatter.2.cloned.1.call-start
  49.1 33.5 %all-gather.2.cloned.1.call-done = bf16[96,16,1024]{2,0,1:T(8,128)(2,1)} async-done(((bf16[96,2,1024]{2,0,1:T(8,128)(2,1)}), bf16[96,16,1024]{2,0,1:T(8,128)(2,1)}) %all-gather.2.cloned.1.call-update) | async-done | bytes 3145744 | tf_op jit(solution)/shard_map/all_gather | solution.py:82
  82.6 3.6 %copy.79 = bf16[96,16,1024]{2,1,0:T(8,128)(2,1)S(1)} copy(bf16[96,16,1024]{2,0,1:T(8,128)(2,1)} %all-gather.2.cloned.1.call-done) | data formatting | bytes 6291456 | tf_op jit(solution)/shard_map/all_gather | solution.py:82
  86.2 3.8 %convolution_convert_fusion = bf16[1536,1024]{0,1:T(8,128)(2,1)S(1)} fusion(bf16[1536,1024]{1,0:T(8,128)(2,1)S(1)} %bitcast.78, bf16[1024,1024]{1,0:T(8,128)(2,1)S(1)} %copy-done), kind=kOutput, calls=%fused_computation.5 | convolution fusion | flops 3222798336 | bytes 8388608 | tf_op jit(solution)/shard_map/dot_general | solution.py:85
  90.1 1.2 convolution_convert_fusion.1
  91.3 1.2 convolution_convert_fusion.2
  92.5 2.1 pad_maximum_fusion
  94.5 6.3 %copy.80 = bf16[1536,1280]{1,0:T(8,128)(2,1)} copy(bf16[1536,1280]{0,1:T(8,128)(2,1)} %pad_maximum_fusion) | data formatting | bytes 7864320 | tf_op jit(solution)/shard_map/concatenate | solution.py:89
  100.9 0.6 copy-done.1
  101.5 0.6 gather_fusion.2
  102.1 0.6 gather_fusion.3
  102.8 0.1 iota_compare_fusion.3
  102.9 0.1 add_convert_fusion.1
  103.0 0.1 iota_compare_fusion.1
  103.0 0.4 multiply_cosine_fusion.1
  103.5 53.5 %reduce-scatter.2.cloned.1.call-done = bf16[12,16,1280]{2,1,0:T(8,128)(2,1)} async-done(((bf16[96,16,1280]{2,1,0:T(8,128)(2,1)}), bf16[12,16,1280]{2,1,0:T(8,128)(2,1)}) %reduce-scatter.2.cloned.1.call-update) | async-done | bytes 491536 | tf_op jit(solution)/shard_map/reduce_scatter | solution.py:88
  157.0 1.1 slice.37
  158.1 0.1 copy.102
  158.3 0.3 fusion.59
  158.6 0.1 convert_element_type.65
  158.7 0.5 fusion.40
  159.1 0.4 fusion.16
  159.5 0.2 pad_maximum_fusion.1
  159.7 0.2 copy-done.4
  160.0 0.7 fusion
  160.7 0.4 fusion.60
  161.0 0.1 fusion.29
  161.1 1.0 fusion.1
  162.2 1.1 fusion.3
  163.2 0.7 fusion.12
  163.9 0.1 copy.121
  164.0 0.2 reshape.416
  164.2 0.1 select_convert_fusion
  164.3 0.2 copy.84
  164.6 19.7 %all_to_all.28 = bf16[12,16,1024]{2,0,1:T(8,128)(2,1)S(1)} all-to-all(bf16[12,16,1024]{2,0,1:T(8,128)(2,1)S(1)} %copy.84), channel_id=1, replica_groups=mesh['grp'=8,'row'=8,'col'=8] {'row'}, dimensions={1} | all-to-all | bytes 786432 | tf_op jit(solution)/shard_map/all_to_all | solution.py:173
  184.3 0.4 copy.97
  184.7 0.4 convolution_convert_fusion.3
  185.1 1.7 copy.88
  186.7 12.2 %all-to-all-start.2 = ((bf16[64,3,2,1024]{3,2,1,0:T(2,128)(2,1)}), bf16[64,3,2,1024]{3,2,1,0:T(2,128)(2,1)S(1)}, u32[]{:S(2)}, u32[]{:S(2)}) async-start(bf16[64,3,2,1024]{3,2,1,0:T(2,128)(2,1)} %bitcast.24), calls=%async_computation.3 | async-start | bytes 1572864 | tf_op jit(solution)/shard_map/all_to_all | solution.py:181
  199.0 22.7 %all-to-all-done.2 = bf16[64,3,2,1024]{3,2,1,0:T(2,128)(2,1)S(1)} async-done(((bf16[64,3,2,1024]{3,2,1,0:T(2,128)(2,1)}), bf16[64,3,2,1024]{3,2,1,0:T(2,128)(2,1)S(1)}, u32[]{:S(2)}, u32[]{:S(2)}) %all-to-all-start.2) | async-done | bytes 786464 | tf_op jit(solution)/shard_map/all_to_all | solution.py:181
  221.7 0.6 fusion.13
  222.2 0.2 copy.91
  222.5 1.0 reshape.419
  (37 shorter events, 0.2 us)
Async XLA Ops:
  6.5 79.7 %copy-start = (bf16[1024,1024]{1,0:T(8,128)(2,1)S(1)}, bf16[1024,1024]{1,0:T(8,128)(2,1)}, u32[]{:S(2)}) copy-start(bf16[1024,1024]{1,0:T(8,128)(2,1)} %param.12) | copy-start | bytes 6291460
  9.3 14.2 %copy-start.7 = (s32[768]{0:T(1024)S(1)}, s32[768]{0:T(1024)}, u32[]{:S(2)}) copy-start(s32[768]{0:T(1024)} %param.17) | copy-start | bytes 9220
  11.8 34.4 %all-to-all-start = ((bf16[64,3,2,1024]{3,2,1,0:T(2,128)(2,1)}), bf16[64,3,2,1024]{3,2,1,0:T(2,128)(2,1)S(1)}, u32[]{:S(2)}, u32[]{:S(2)}) async-start(bf16[64,3,2,1024]{3,2,1,0:T(2,128)(2,1)} %copy.77), calls=%async_computation | async-start | bytes 1572864 | tf_op jit(solution)/shard_map/all_to_all | solution.py:70
  23.4 59.2 %all-gather.2.cloned.1.call-start = ((), (), s32[]{:S(2)}) async-start(), calls=%async_computation.4 | async-start | bytes 3538944 | tf_op jit(solution)/shard_map/all_gather | solution.py:82
  48.8 108.1 %reduce-scatter.2.cloned.1.call-start = ((), (), s32[]{:S(2)}) async-start(), calls=%async_computation.5 | async-start | bytes 4423680 | tf_op jit(solution)/shard_map/reduce_scatter | solution.py:88
  86.2 3.8 %copy-start.5 = (bf16[1024,128]{1,0:T(8,128)(2,1)S(1)}, bf16[1024,128]{1,0:T(8,128)(2,1)}, u32[]{:S(2)}) copy-start(bf16[1024,128]{1,0:T(8,128)(2,1)} %param.14) | copy-start | bytes 786436
  90.1 1.2 copy-start.6
  100.8 0.7 copy-start.1
  100.8 1.3 copy-start.2
  157.0 1.6 copy-start.3
  158.5 1.4 copy-start.4
  160.6 1.5 copy-start.8
  186.7 34.9 %all-to-all-start.2 = ((bf16[64,3,2,1024]{3,2,1,0:T(2,128)(2,1)}), bf16[64,3,2,1024]{3,2,1,0:T(2,128)(2,1)S(1)}, u32[]{:S(2)}, u32[]{:S(2)}) async-start(bf16[64,3,2,1024]{3,2,1,0:T(2,128)(2,1)} %bitcast.24), calls=%async_computation.3 | async-start | bytes 1572864 | tf_op jit(solution)/shard_map/all_to_all | solution.py:181
Sparse Core Ops, SparseCore 0:
  49.0 33.5 all-gather.1
  100.9 55.9 reduce-scatter.1
where the time goes:
time: 231 us; the launch traced here: 230 us
  waiting for transfers between devices  127 us (55%)
  local copies, waits for them, and re-layouts  24.5 us (11%)
  starting transfers between devices  24.1 us (10%)
  blocking collectives  19.7 us (9%)
  between operations  13.8 us (6%)
  other arithmetic  11.2 us (5%)
  matrix products  10.2 us (4%)
    reduce_scatter x1, waiting for transfers between devices, local(): lax.psum_scatter(jnp.concatenate([query_part, key_part, value_part], axis...  53.5 us
    all_gather x1, waiting for transfers between devices, local(): tokens = lax.all_gather(landed, 'col', axis=1, tiled=True)  33.5 us
    all_to_all x1, waiting for transfers between devices, local(): lax.all_to_all(returning.reshape(regions, capacity, slot_share, query_wid...  22.7 us
    all_to_all x1, blocking collectives, local(): lax.all_to_all(result, 'row', split_axis=1, concat_axis=0, tiled=True)  19.7 us
    all_to_all x1, waiting for transfers between devices, local(): lax.all_to_all(outgoing.reshape(regions, capacity, slot_width, feature_wi...  17.1 us
    all_to_all x1, starting transfers between devices, local(): lax.all_to_all(returning.reshape(regions, capacity, slot_share, query_wid...  12.2 us
    all_to_all x1, starting transfers between devices, local(): lax.all_to_all(outgoing.reshape(regions, capacity, slot_width, feature_wi...  11.6 us
    concatenate x1, local copies, waits for them, and re-layouts, local(): jnp.concatenate([query_part, key_part, value_part], axis=1)  6.26 us
  transfers between devices with their start and end apart: 4, of which 4 were waited for; matrix products, arithmetic and copies ran while one was open for 3% of the time, Pallas kernels for 0%

commit v1 on v0

--- a/solution.py
+++ b/solution.py
@@ -79,7 +79,23 @@
     landed = jnp.take(
         arrived.reshape(regions * capacity, slot_width, feature_width), source_row, axis=0
     )
-    tokens = lax.all_gather(landed, "col", axis=1, tiled=True)
+    size, here, span = (lax.axis_size("col"), lax.axis_index("col"), landed.shape[1])
+    right = [(i, (i + 1) % size) for i in range(size)]
+    left = [(i, (i - 1) % size) for i in range(size)]
+    tokens = jnp.zeros((*landed.shape[:1], size * span, *landed.shape[1 + 1 :]), landed.dtype)
+    tokens = lax.dynamic_update_slice_in_dim(tokens, landed, here * span, axis=1)
+    from_left = from_right = landed
+    middle = size // 2
+    for step in range(1, middle + 1):
+        from_left = lax.ppermute(from_left, "col", right)
+        tokens = lax.dynamic_update_slice_in_dim(
+            tokens, from_left, (here - step) % size * span, axis=1
+        )
+        if step < size - middle:
+            from_right = lax.ppermute(from_right, "col", left)
+            tokens = lax.dynamic_update_slice_in_dim(
+                tokens, from_right, (here + step) % size * span, axis=1
+            )
     agents_here = cache_keys.shape[0]
     picked = tokens.reshape(lax.axis_size("row") * agents_here * slot_count, feature_width)
     query_part = jnp.dot(picked, query_weight, preferred_element_type=jnp.float32)

time: 231 us -> 236 us (1.022)
  waiting for transfers between devices: 127 us -> 108 us
  starting transfers between devices: 24.1 us -> 33.8 us
  local copies, waits for them, and re-layouts: 24.5 us -> 31.7 us
  matrix products: 10.2 us -> 15.9 us
    all_gather x1 -> x0, waiting for transfers between devices: 33.5 us -> none  [local(): tokens = lax.all_gather(landed, 'col', axis=1, tiled=True)]
    ppermute x0 -> x7, starting transfers between devices: none -> 10.1 us  [the longest x4 8.75 us: local(): from_left = lax.ppermute(from_left, 'col', right)]
    ppermute x0 -> x7, waiting for transfers between devices: none -> 9.85 us  [the longest x4 9.74 us: local(): from_left = lax.ppermute(from_left, 'col', right)]
    dynamic_update_slice x0 -> x7, local copies, waits for them, and re-layouts: none -> 9.56 us  [the longest x4 5.3 us: local(): lax.dynamic_update_slice_in_dim(tokens, from_left, (here - step) % size *...]
    reduce_scatter x1, waiting for transfers between devices: 53.5 us -> 58.5 us  [local(): lax.psum_scatter(jnp.concatenate([query_part, key_part, value_part], axis...]
    all_gather x1 -> x0, local copies, waits for them, and re-layouts: 3.61 us -> none  [local(): tokens = lax.all_gather(landed, 'col', axis=1, tiled=True)]
  transfers between devices with their start and end apart: 4 -> 10, of which waited for: 4 -> 7; matrix products, arithmetic and copies ran while one was open for 3% -> 7% of each run, Pallas kernels for 0% -> 0%
where the time goes in v1:
time: 236 us; the launch traced here: 235 us
  waiting for transfers between devices  108 us (46%)
  starting transfers between devices  33.8 us (14%)
  local copies, waits for them, and re-layouts  31.7 us (13%)
  blocking collectives  19.7 us (8%)
  matrix products  15.9 us (7%)
  between operations  13.8 us (6%)
  other arithmetic  12.1 us (5%)
    reduce_scatter x1, waiting for transfers between devices, local(): lax.psum_scatter(jnp.concatenate([query_part, key_part, value_part], axis...  58.5 us
    all_to_all x1, waiting for transfers between devices, local(): lax.all_to_all(returning.reshape(regions, capacity, slot_share, query_wid...  22.7 us
    all_to_all x1, blocking collectives, local(): lax.all_to_all(result, 'row', split_axis=1, concat_axis=0, tiled=True)  19.7 us
    all_to_all x1, waiting for transfers between devices, local(): lax.all_to_all(outgoing.reshape(regions, capacity, slot_width, feature_wi...  17.1 us
    all_to_all x1, starting transfers between devices, local(): lax.all_to_all(returning.reshape(regions, capacity, slot_share, query_wid...  12.1 us
    all_to_all x1, starting transfers between devices, local(): lax.all_to_all(outgoing.reshape(regions, capacity, slot_width, feature_wi...  11.6 us
    ppermute x4, waiting for transfers between devices, local(): from_left = lax.ppermute(from_left, 'col', right)  9.74 us
    ppermute x4, starting transfers between devices, local(): from_left = lax.ppermute(from_left, 'col', right)  8.75 us
  transfers between devices with their start and end apart: 10, of which 7 were waited for; matrix products, arithmetic and copies ran while one was open for 7% of the time, Pallas kernels for 0%

profile of v1, /device:TPU:1, one launch (start us, length us, event | category | flops | bytes accessed | tf_op | source)
XLA Modules:
  0.0 235.3 jit_solution(7905800962975157471)
XLA Ops:
  6.5 0.8 add_select_fusion
  7.6 0.1 convert_reduce_fusion
  8.1 1.2 copy.75
  9.3 0.3 fusion.11
  9.7 0.4 copy.102
  10.1 1.7 copy.59
  11.8 11.6 %all-to-all-start = ((bf16[64,3,2,1024]{3,2,1,0:T(2,128)(2,1)}), bf16[64,3,2,1024]{3,2,1,0:T(2,128)(2,1)S(1)}, u32[]{:S(2)}, u32[]{:S(2)}) async-start(bf16[64,3,2,1024]{3,2,1,0:T(2,128)(2,1)} %copy.59), calls=%async_computation | async-start | bytes 1572864 | tf_op jit(solution)/shard_map/all_to_all | solution.py:70
  23.5 4.4 %sort.17 = (s32[768]{0:T(1024)}, s32[768]{0:T(1024)S(1)}) sort(s32[768]{0:T(1024)S(1)} %copy-done.8, s32[768]{0:T(1024)S(1)} %iota.103), dimensions={0}, to_apply=%region_0.1 | sort | flops 7680 | bytes 12288 | tf_op jit(solution)/shard_map/jit(argsort)/sort | solution.py:58
  27.9 1.0 gather_fusion
  29.0 17.1 %all-to-all-done = bf16[64,3,2,1024]{3,2,1,0:T(2,128)(2,1)S(1)} async-done(((bf16[64,3,2,1024]{3,2,1,0:T(2,128)(2,1)}), bf16[64,3,2,1024]{3,2,1,0:T(2,128)(2,1)S(1)}, u32[]{:S(2)}, u32[]{:S(2)}) %all-to-all-start) | async-done | bytes 786464 | tf_op jit(solution)/shard_map/all_to_all | solution.py:70
  46.2 1.4 gather_fusion.1
  47.5 2.0 broadcast_in_dim.101
  49.6 1.3 constant_dynamic-update-slice_fusion.7
  50.9 2.1 collective-permute-start
  53.0 4.7 %collective-permute-done = bf16[96,2,1024]{2,1,0:T(2,128)(2,1)S(1)} collective-permute-done((bf16[96,2,1024]{2,1,0:T(2,128)(2,1)S(1)}, bf16[96,2,1024]{2,1,0:T(2,128)(2,1)S(1)}, u32[]{:S(2)}, u32[]{:S(2)}) %collective-permute-start) | collective-permute-done | bytes 393248 | tf_op jit(solution)/shard_map/ppermute | solution.py:90
  57.7 2.5 %collective-permute-start.2 = (bf16[96,2,1024]{2,1,0:T(2,128)(2,1)S(1)}, bf16[96,2,1024]{2,1,0:T(2,128)(2,1)S(1)}, u32[]{:S(2)}, u32[]{:S(2)}) collective-permute-start(bf16[96,2,1024]{2,1,0:T(2,128)(2,1)S(1)} %collective-permute-done), channel_id=1, source_target_pairs={{0,1},{1,2},{2,3},{3,4},{4,5},{5,6},{6,7},{7,0},{8,9},{9,10},{10,1... | collective-permute-start | bytes 1179656 | tf_op jit(solution)/shard_map/ppermute | solution.py:90
  60.3 4.6 %collective-permute-done.2 = bf16[96,2,1024]{2,1,0:T(2,128)(2,1)S(1)} collective-permute-done((bf16[96,2,1024]{2,1,0:T(2,128)(2,1)S(1)}, bf16[96,2,1024]{2,1,0:T(2,128)(2,1)S(1)}, u32[]{:S(2)}, u32[]{:S(2)}) %collective-permute-start.2) | collective-permute-done | bytes 393248 | tf_op jit(solution)/shard_map/ppermute | solution.py:90
  64.9 2.5 %collective-permute-start.4 = (bf16[96,2,1024]{2,1,0:T(2,128)(2,1)S(1)}, bf16[96,2,1024]{2,1,0:T(2,128)(2,1)S(1)}, u32[]{:S(2)}, u32[]{:S(2)}) collective-permute-start(bf16[96,2,1024]{2,1,0:T(2,128)(2,1)S(1)} %collective-permute-done.2), channel_id=1, source_target_pairs={{0,1},{1,2},{2,3},{3,4},{4,5},{5,6},{6,7},{7,0},{8,9},{9,10},{10,1... | collective-permute-start | bytes 1179656 | tf_op jit(solution)/shard_map/ppermute | solution.py:90
  67.4 2.1 constant_dynamic-update-slice_fusion.6
  69.5 1.3 collective-permute-start.5
  70.8 2.1 constant_dynamic-update-slice_fusion.5
  72.9 1.7 collective-permute-start.6
  74.6 1.1 constant_dynamic-update-slice_fusion.4
  75.7 1.1 constant_dynamic-update-slice_fusion.3
  76.8 1.1 constant_dynamic-update-slice_fusion.2
  77.8 1.1 constant_dynamic-update-slice_fusion.1
  78.9 0.4 collective-permute-done.6
  79.3 1.1 constant_dynamic-update-slice_fusion
  80.4 5.7 %convolution_convert_fusion = bf16[1536,1024]{0,1:T(8,128)(2,1)S(1)} fusion(bf16[1536,1024]{1,0:T(8,128)(2,1)} %bitcast.8, bf16[1024,1024]{1,0:T(8,128)(2,1)S(1)} %copy-done), kind=kOutput, calls=%fused_computation.5 | convolution fusion | flops 3222798336 | bytes 8388608 | tf_op jit(solution)/shard_map/dot_general | solution.py:101
  86.1 3.1 %convolution_convert_fusion.1 = bf16[1536,128]{0,1:T(8,128)(2,1)S(1)} fusion(bf16[1536,1024]{1,0:T(8,128)(2,1)} %bitcast.8, bf16[1024,128]{1,0:T(8,128)(2,1)S(1)} %copy-done.6), kind=kOutput, calls=%fused_computation.9 | convolution fusion | flops 402849792 | bytes 3801088 | tf_op jit(solution)/shard_map/dot_general | solution.py:103
  89.2 3.1 %convolution_convert_fusion.2 = bf16[1536,128]{0,1:T(8,128)(2,1)S(1)} fusion(bf16[1536,1024]{1,0:T(8,128)(2,1)} %bitcast.8, bf16[1024,128]{1,0:T(8,128)(2,1)S(1)} %copy-done.7), kind=kOutput, calls=%fused_computation.10 | convolution fusion | flops 402849792 | bytes 3801088 | tf_op jit(solution)/shard_map/dot_general | solution.py:102
  92.3 2.1 pad_maximum_fusion
  94.4 6.3 %copy.60 = bf16[1536,1280]{1,0:T(8,128)(2,1)} copy(bf16[1536,1280]{0,1:T(8,128)(2,1)} %pad_maximum_fusion) | data formatting | bytes 7864320 | tf_op jit(solution)/shard_map/concatenate | solution.py:105
  100.8 0.6 copy-done.1
  101.4 0.6 gather_fusion.2
  102.1 0.6 gather_fusion.3
  103.0 0.4 multiply_cosine_fusion.1
  103.4 58.5 %reduce-scatter.2.cloned.1.call-done = bf16[12,16,1280]{2,1,0:T(8,128)(2,1)} async-done(((bf16[96,16,1280]{2,1,0:T(8,128)(2,1)}), bf16[12,16,1280]{2,1,0:T(8,128)(2,1)}) %reduce-scatter.2.cloned.1.call-update) | async-done | bytes 491536 | tf_op jit(solution)/shard_map/reduce_scatter | solution.py:104
  162.0 1.1 slice.37
  163.1 0.1 copy.82
  163.3 0.3 fusion.59
  163.7 0.5 fusion.40
  164.1 0.4 fusion.16
  164.5 0.2 pad_maximum_fusion.1
  164.7 0.2 copy-done.4
  165.0 0.7 fusion
  165.6 0.4 fusion.60
  166.0 0.1 fusion.29
  166.1 1.0 fusion.1
  167.2 1.1 fusion.3
  168.2 0.7 fusion.12
  168.9 0.1 copy.101
  169.0 0.2 reshape.416
  169.2 0.1 select_convert_fusion
  169.3 0.2 copy.64
  169.6 19.7 %all_to_all.28 = bf16[12,16,1024]{2,0,1:T(8,128)(2,1)S(1)} all-to-all(bf16[12,16,1024]{2,0,1:T(8,128)(2,1)S(1)} %copy.64), channel_id=1, replica_groups=mesh['grp'=8,'row'=8,'col'=8] {'row'}, dimensions={1} | all-to-all | bytes 786432 | tf_op jit(solution)/shard_map/all_to_all | solution.py:189
  189.3 0.4 copy.77
  189.7 0.4 convolution_convert_fusion.3
  190.1 1.7 copy.68
  191.8 12.1 %all-to-all-start.2 = ((bf16[64,3,2,1024]{3,2,1,0:T(2,128)(2,1)}), bf16[64,3,2,1024]{3,2,1,0:T(2,128)(2,1)S(1)}, u32[]{:S(2)}, u32[]{:S(2)}) async-start(bf16[64,3,2,1024]{3,2,1,0:T(2,128)(2,1)} %bitcast.24), calls=%async_computation.3 | async-start | bytes 1572864 | tf_op jit(solution)/shard_map/all_to_all | solution.py:197
  203.9 22.7 %all-to-all-done.2 = bf16[64,3,2,1024]{3,2,1,0:T(2,128)(2,1)S(1)} async-done(((bf16[64,3,2,1024]{3,2,1,0:T(2,128)(2,1)}), bf16[64,3,2,1024]{3,2,1,0:T(2,128)(2,1)S(1)}, u32[]{:S(2)}, u32[]{:S(2)}) %all-to-all-start.2) | async-done | bytes 786464 | tf_op jit(solution)/shard_map/all_to_all | solution.py:197
  226.7 0.6 fusion.13
  227.2 0.2 copy.71
  227.4 1.0 reshape.419
  (56 shorter events, 1.3 us)
Async XLA Ops:
  6.5 73.9 %copy-start = (bf16[1024,1024]{1,0:T(8,128)(2,1)S(1)}, bf16[1024,1024]{1,0:T(8,128)(2,1)}, u32[]{:S(2)}) copy-start(bf16[1024,1024]{1,0:T(8,128)(2,1)} %param.12) | copy-start | bytes 6291460
  9.3 14.2 %copy-start.8 = (s32[768]{0:T(1024)S(1)}, s32[768]{0:T(1024)}, u32[]{:S(2)}) copy-start(s32[768]{0:T(1024)} %param.17) | copy-start | bytes 9220
  11.8 34.4 %all-to-all-start = ((bf16[64,3,2,1024]{3,2,1,0:T(2,128)(2,1)}), bf16[64,3,2,1024]{3,2,1,0:T(2,128)(2,1)S(1)}, u32[]{:S(2)}, u32[]{:S(2)}) async-start(bf16[64,3,2,1024]{3,2,1,0:T(2,128)(2,1)} %copy.59), calls=%async_computation | async-start | bytes 1572864 | tf_op jit(solution)/shard_map/all_to_all | solution.py:70
  23.4 138.5 %reduce-scatter.2.cloned.1.call-start = ((), (), s32[]{:S(2)}) async-start(), calls=%async_computation.4 | async-start | bytes 4423680 | tf_op jit(solution)/shard_map/reduce_scatter | solution.py:104
  50.9 6.8 %collective-permute-start = (bf16[96,2,1024]{2,1,0:T(2,128)(2,1)S(1)}, bf16[96,2,1024]{2,1,0:T(2,128)(2,1)S(1)}, u32[]{:S(2)}, u32[]{:S(2)}) collective-permute-start(bf16[96,2,1024]{2,1,0:T(2,128)(2,1)S(1)} %get-tuple-element.9), channel_id=1, source_target_pairs={{0,1},{1,2},{2,3},{3,4},{4,5},{5,6},{6,7},{7,0},{8,9},{9,10},{10,1... | collective-permute-start | bytes 1179656 | tf_op jit(solution)/shard_map/ppermute | solution.py:90
  53.0 7.3 %collective-permute-start.1 = (bf16[96,2,1024]{2,1,0:T(2,128)(2,1)S(1)}, bf16[96,2,1024]{2,1,0:T(2,128)(2,1)}, u32[]{:S(2)}, u32[]{:S(2)}) collective-permute-start(bf16[96,2,1024]{2,1,0:T(2,128)(2,1)S(1)} %get-tuple-element.9), channel_id=1, source_target_pairs={{0,7},{1,0},{2,1},{3,2},{4,3},{5,4},{6,5},{7,6},{8,15},{9,8},{10,9... | collective-permute-start | bytes 1179656 | tf_op jit(solution)/shard_map/ppermute | solution.py:95
  57.7 7.2 %copy-start.5 = (bf16[96,2,1024]{2,1,0:T(2,128)(2,1)}, bf16[96,2,1024]{2,1,0:T(2,128)(2,1)S(1)}, u32[]{:S(2)}) copy-start(bf16[96,2,1024]{2,1,0:T(2,128)(2,1)S(1)} %collective-permute-done) | copy-start | bytes 1179652
  57.7 7.2 %collective-permute-start.2 = (bf16[96,2,1024]{2,1,0:T(2,128)(2,1)S(1)}, bf16[96,2,1024]{2,1,0:T(2,128)(2,1)S(1)}, u32[]{:S(2)}, u32[]{:S(2)}) collective-permute-start(bf16[96,2,1024]{2,1,0:T(2,128)(2,1)S(1)} %collective-permute-done), channel_id=1, source_target_pairs={{0,1},{1,2},{2,3},{3,4},{4,5},{5,6},{6,7},{7,0},{8,9},{9,10},{10,1... | collective-permute-start | bytes 1179656 | tf_op jit(solution)/shard_map/ppermute | solution.py:90
  60.3 9.2 %collective-permute-start.3 = (bf16[96,2,1024]{2,1,0:T(2,128)(2,1)}, bf16[96,2,1024]{2,1,0:T(2,128)(2,1)S(1)}, u32[]{:S(2)}, u32[]{:S(2)}) collective-permute-start(bf16[96,2,1024]{2,1,0:T(2,128)(2,1)} %collective-permute-done.1), channel_id=1, source_target_pairs={{0,7},{1,0},{2,1},{3,2},{4,3},{5,4},{6,5},{7,6},{8,15},{9,8},{10,9... | collective-permute-start | bytes 1179656 | tf_op jit(solution)/shard_map/ppermute | solution.py:95
  64.9 8.0 %collective-permute-start.4 = (bf16[96,2,1024]{2,1,0:T(2,128)(2,1)S(1)}, bf16[96,2,1024]{2,1,0:T(2,128)(2,1)S(1)}, u32[]{:S(2)}, u32[]{:S(2)}) collective-permute-start(bf16[96,2,1024]{2,1,0:T(2,128)(2,1)S(1)} %collective-permute-done.2), channel_id=1, source_target_pairs={{0,1},{1,2},{2,3},{3,4},{4,5},{5,6},{6,7},{7,0},{8,9},{9,10},{10,1... | collective-permute-start | bytes 1179656 | tf_op jit(solution)/shard_map/ppermute | solution.py:90
  69.5 8.3 %collective-permute-start.5 = (bf16[96,2,1024]{2,1,0:T(2,128)(2,1)S(1)}, bf16[96,2,1024]{2,1,0:T(2,128)(2,1)S(1)}, u32[]{:S(2)}, u32[]{:S(2)}) collective-permute-start(bf16[96,2,1024]{2,1,0:T(2,128)(2,1)S(1)} %collective-permute-done.3), channel_id=1, source_target_pairs={{0,7},{1,0},{2,1},{3,2},{4,3},{5,4},{6,5},{7,6},{8,15},{9,8},{10,9... | collective-permute-start | bytes 1179656 | tf_op jit(solution)/shard_map/ppermute | solution.py:95
  72.9 6.4 %collective-permute-start.6 = (bf16[96,2,1024]{2,1,0:T(2,128)(2,1)S(1)}, bf16[96,2,1024]{2,1,0:T(2,128)(2,1)S(1)}, u32[]{:S(2)}, u32[]{:S(2)}) collective-permute-start(bf16[96,2,1024]{2,1,0:T(2,128)(2,1)S(1)} %collective-permute-done.4), channel_id=1, source_target_pairs={{0,1},{1,2},{2,3},{3,4},{4,5},{5,6},{6,7},{7,0},{8,9},{9,10},{10,1... | collective-permute-start | bytes 1179656 | tf_op jit(solution)/shard_map/ppermute | solution.py:90
  80.4 5.7 %copy-start.6 = (bf16[1024,128]{1,0:T(8,128)(2,1)S(1)}, bf16[1024,128]{1,0:T(8,128)(2,1)}, u32[]{:S(2)}) copy-start(bf16[1024,128]{1,0:T(8,128)(2,1)} %param.14) | copy-start | bytes 786436
  86.1 3.1 %copy-start.7 = (bf16[1024,128]{1,0:T(8,128)(2,1)S(1)}, bf16[1024,128]{1,0:T(8,128)(2,1)}, u32[]{:S(2)}) copy-start(bf16[1024,128]{1,0:T(8,128)(2,1)} %param.13) | copy-start | bytes 786436
  100.7 0.7 copy-start.1
  100.7 1.3 copy-start.2
  161.9 1.6 copy-start.3
  163.5 1.4 copy-start.4
  165.6 1.5 copy-start.9
  191.8 34.9 %all-to-all-start.2 = ((bf16[64,3,2,1024]{3,2,1,0:T(2,128)(2,1)}), bf16[64,3,2,1024]{3,2,1,0:T(2,128)(2,1)S(1)}, u32[]{:S(2)}, u32[]{:S(2)}) async-start(bf16[64,3,2,1024]{3,2,1,0:T(2,128)(2,1)} %bitcast.24), calls=%async_computation.3 | async-start | bytes 1572864 | tf_op jit(solution)/shard_map/all_to_all | solution.py:197
Sparse Core Ops, SparseCore 0:
  100.9 61.0 reduce-scatter.1
